TPU v7x, 128 devices: a whole 4x4x4 slice. The times are simulated.
128 devices in a mesh: row: 8 (over x, z_lo), col: 16 (over z_hi, y, core).
Axes of the slice: x: 4, y: 4, z: 4 (z_hi: 2, z_lo: 2; z = z_hi * 2 + z_lo), core: 2. Of those that a mesh axis runs over, the one named last changes fastest.
Arguments:
- thermal_field_values: float32 [256, 1024, 1024], P('col', 'row'), may hold values from -6 to 6
- particle_entry_location: int32 [3, 8388608], P(None, ('row', 'col')), may hold values from 0 to 1023, as said below
- particle_condensation_energy: float32 [8388608], P(('row', 'col')), may hold values from -96 to 96
- tube_particle_tally: int32 [128], P(('row', 'col')), may hold values from 16384 to 65536, as said below
- eigen_decay_factors: float32 [256], replicated, may hold values from 0.05 to 2
- stratum_eigen_analysis: bfloat16 [256, 256], replicated, may hold values from -0.375 to 0.375
- eigen_synthesis_matrix: bfloat16 [256, 256], replicated, may hold values from -0.375 to 0.375
Outputs:
- updated: float32 [256, 1024, 1024], P('col', 'row')
Inputs may be any that keep to these rules, and one draw needn't show every extreme that they name: particle_entry_location[0] lies below 1024, particle_entry_location[1] below 128, particle_entry_location[2] below 16, for every slot, padding slots too. `tube_particle_tally`: at least one pencil is full.
All inputs are finite; a program needn't handle non-finite values.
Results may differ from a plain program's by a relative error of at most 0.011.
Values may be sent and summed in bfloat16 or wider, within the bound.
A program may use at most 128 MiB of HBM per device.

v0:
```python
import math

import jax
import jax.numpy as jnp
from jax import lax
from jax.sharding import PartitionSpec as P

DIFFUSION = 0.1


def with_halo(array, sides, width):
    for axis, dim in sides:
        devices, length = (lax.axis_size(axis), array.shape[dim])
        up = [(i, (i + 1) % devices) for i in range(devices)]
        down = [(j, i) for i, j in up]
        last = lax.slice_in_dim(array, length - width, length, axis=dim)
        first = lax.slice_in_dim(array, 0, width, axis=dim)
        before = lax.ppermute(last, axis, up)
        after = lax.ppermute(first, axis, down)
        array = jnp.concatenate([before, array, after], axis=dim)
    return array


def cas_table(row_index, col_index, length):
    product = row_index[:, None] * col_index[None, :] % length
    angle = product.astype(jnp.float32) * (2.0 * math.pi / length)
    return ((jnp.cos(angle) + jnp.sin(angle)) * (1.0 / math.sqrt(length))).astype(jnp.bfloat16)


def wave_square(index, length):
    folded = jnp.minimum(index, length - index).astype(jnp.float32)
    return (folded * (2.0 * math.pi / length)) ** 2


def body(
    thermal_field_values,
    particle_entry_location,
    particle_condensation_energy,
    tube_particle_tally,
    eigen_decay_factors,
    stratum_eigen_analysis,
    eigen_synthesis_matrix,
):
    tile_stratum_span, tile_lateral_span, periodic_box_length = thermal_field_values.shape
    row_index = lax.axis_index("row")
    col_index = lax.axis_index("col")
    row_count = lax.axis_size("row")
    col_count = lax.axis_size("col")
    total_y = tile_lateral_span * row_count
    total_z = tile_stratum_span * col_count
    slots = particle_condensation_energy.shape[0]
    live = jnp.arange(slots, dtype=jnp.int32) < tube_particle_tally[0]
    flat = (
        particle_entry_location[2] * tile_lateral_span + particle_entry_location[1]
    ) * periodic_box_length + particle_entry_location[0]
    deposit = jax.ops.segment_sum(
        jnp.where(live, particle_condensation_energy, 0.0),
        flat,
        num_segments=tile_stratum_span * tile_lateral_span * periodic_box_length,
    ).reshape(tile_stratum_span, tile_lateral_span, periodic_box_length)
    padded = with_halo(deposit, (("row", 1), ("col", 0)), 1)
    plane = jnp.arange(tile_stratum_span + 2, dtype=jnp.int32)
    wall = (plane == 0) & (col_index == 0) | (plane == tile_stratum_span + 1) & (
        col_index == col_count - 1
    )
    padded = jnp.where(wall[:, None, None], 0.0, padded)
    along_z = 0.25 * (padded[:-2] + padded[2:]) + 0.5 * padded[1:-1]
    along_y = 0.25 * (along_z[:, :-2] + along_z[:, 2:]) + 0.5 * along_z[:, 1:-1]
    condensation_warming = (
        0.25 * (jnp.roll(along_y, 1, 2) + jnp.roll(along_y, -1, 2)) + 0.5 * along_y
    )
    thermal_source_term = (thermal_field_values + condensation_warming).astype(jnp.bfloat16)
    index_x = jnp.arange(periodic_box_length, dtype=jnp.int32)
    index_y = jnp.arange(total_y, dtype=jnp.int32)
    table_x = cas_table(index_x, index_x, periodic_box_length)
    table_y = cas_table(index_y, index_y, total_y)
    row_block = periodic_box_length // row_count
    along_x = jnp.dot(thermal_source_term, table_x, preferred_element_type=jnp.float32).astype(
        jnp.bfloat16
    )
    gathered_y = lax.all_to_all(along_x, "row", split_axis=2, concat_axis=1, tiled=True)
    spectrum = jnp.einsum(
        "zyk,ym->zmk", gathered_y, table_y, preferred_element_type=jnp.float32
    ).astype(jnp.bfloat16)
    columns = lax.all_to_all(spectrum, "col", split_axis=1, concat_axis=0, tiled=True)
    col_block = columns.shape[1]
    modal = jnp.dot(
        stratum_eigen_analysis, columns.reshape(total_z, -1), preferred_element_type=jnp.float32
    ).reshape(total_z, col_block, row_block)
    wave_y = col_index * col_block + jnp.arange(col_block, dtype=jnp.int32)
    wave_x = row_index * row_block + jnp.arange(row_block, dtype=jnp.int32)
    denom = (
        1.0
        + DIFFUSION
        * (
            wave_square(wave_y, total_y)[None, :, None]
            + wave_square(wave_x, periodic_box_length)[None, None, :]
        )
        + eigen_decay_factors[:, None, None]
    )
    scaled = (modal / denom).astype(jnp.bfloat16)
    levels = (
        jnp.dot(
            eigen_synthesis_matrix, scaled.reshape(total_z, -1), preferred_element_type=jnp.float32
        )
        .astype(jnp.bfloat16)
        .reshape(total_z, col_block, row_block)
    )
    returned = lax.all_to_all(levels, "col", split_axis=0, concat_axis=1, tiled=True)
    back_y = jnp.einsum(
        "zmk,my->zyk", returned, table_y, preferred_element_type=jnp.float32
    ).astype(jnp.bfloat16)
    pencil_home = lax.all_to_all(back_y, "row", split_axis=1, concat_axis=2, tiled=True)
    return jnp.dot(pencil_home, table_x, preferred_element_type=jnp.float32)


def solution(mesh):
    in_specs = (
        P("col", "row", None),
        P(None, ("row", "col")),
        P(("row", "col")),
        P(("row", "col")),
        P(),
        P(),
        P(),
    )
    out_specs = P("col", "row", None)
    return jax.shard_map(body, mesh=mesh, in_specs=in_specs, out_specs=out_specs, check_vma=False)
```

profile of v0, /device:TPU:1, one launch (start us, length us, event | category | flops | bytes accessed | tf_op | source)
XLA Modules:
  0.0 777.0 jit_solution(4925600848910518133)
XLA Ops:
  0.0 0.0 copy-start
  0.7 2.9 slice_add_fusion.2
  3.6 1.0 fusion.45
  4.6 345.4 %scatter_custom_fusion = f32[2097152]{0:T(1024)} fusion(s32[65536]{0:T(1024)S(1)} %bitcast.76, f32[65536]{0:T(1024)S(1)} %fusion.45, f32[]{:T(128)} %constant.25.clone.1), kind=kCustom, calls=%fused_computation.30 | custom fusion | flops 65536 | bytes 8388612 | tf_op jit(solution)/shard_map/scatter-add | solution.py:56
  349.9 9.3 %reshape.113 = f32[16,128,1024]{2,1,0:T(8,128)} reshape(f32[2097152]{0:T(1024)} %scatter_custom_fusion) | data formatting | bytes 16777216 | tf_op jit(solution)/shard_map/reshape | solution.py:60
  359.2 1.3 fusion.79
  360.5 2.5 collective-permute-start
  363.1 2.3 collective-permute-start.1
  365.3 1.6 collective-permute-done
  366.9 0.0 collective-permute-done.1
  366.9 1.3 pad_maximum_fusion.2
  368.2 3.3 collective-permute-start.2
  371.6 0.0 collective-permute-start.3
  371.6 6.5 collective-permute-done.2
  378.1 2.8 collective-permute-done.3
  380.8 6.5 maximum_select_fusion
  387.4 4.3 fusion
  391.7 2.2 fusion.4
  393.9 5.1 fusion.77
  399.0 0.4 fusion.78
  399.4 29.7 %fusion.22 = bf16[16,128,1024]{2,1,0:T(8,128)(2,1)} fusion(f32[16,128,1024]{2,1,0:T(8,128)} %param.7, f32[16,128,1023]{2,1,0:T(8,128)} %get-tuple-element.8, f32[16,128,1]{2,1,0:T(8,128)S(1)} %get-tuple-element.10, f32[16,128,1]{2,1,0:T(8,128)S(1)} %get-tuple-element.9, f32[16,128,1023]{2,1,0:T(8,128)S(1)} %get-tuple-element.7, f32[16,128,1024]{2,1,0:T(8,128)S(1)} %fusion.4), kind=kOutput, calls=%fused_computation.37 | convolution fusion | flops 4331667456 | bytes 37748736 | tf_op jit(solution)/shard_map/dot_general | solution.py:78
  429.1 6.8 copy.20
  435.9 52.0 %all_to_all.69 = bf16[16,128,1024]{1,0,2:T(8,128)(2,1)} all-to-all(bf16[16,128,1024]{1,0,2:T(8,128)(2,1)} %copy.20), channel_id=1, replica_groups=mesh['row'=8,'col'=16] {'row'}, dimensions={2} | all-to-all | bytes 8388608 | tf_op jit(solution)/shard_map/all_to_all | solution.py:81
  487.9 6.6 copy.21
  494.4 23.3 %convert_bitcast_fusion.1 = bf16[16,1024,128]{2,1,0:T(8,128)(2,1)S(1)} fusion(bf16[16,1024,128]{2,1,0:T(8,128)(2,1)} %bitcast.74), kind=kOutput, calls=%fused_computation.29 | convolution fusion | flops 4314890240 | bytes 8388608 | tf_op jit(solution)/shard_map/zyk,ym->zmk/dot_general | solution.py:82
  517.7 4.7 copy.23
  522.4 10.2 %all-to-all-start.1 = ((bf16[16,1024,128]{2,0,1:T(8,128)(2,1)}), bf16[16,1024,128]{2,0,1:T(8,128)(2,1)}, u32[]{:S(2)}, u32[]{:S(2)}) async-start(bf16[16,1024,128]{2,0,1:T(8,128)(2,1)} %copy.23), calls=%async_computation.1 | async-start | bytes 8388608 | tf_op jit(solution)/shard_map/all_to_all | solution.py:85
  532.7 0.1 add.152
  532.8 55.7 %all-to-all-done.1 = bf16[16,1024,128]{2,0,1:T(8,128)(2,1)} async-done(((bf16[16,1024,128]{2,0,1:T(8,128)(2,1)}), bf16[16,1024,128]{2,0,1:T(8,128)(2,1)}, u32[]{:S(2)}, u32[]{:S(2)}) %all-to-all-start.1) | async-done | bytes 4194336 | tf_op jit(solution)/shard_map/all_to_all | solution.py:85
  588.6 0.0 copy-start.1
  588.6 0.0 copy-start.2
  588.6 5.3 copy.24
  593.9 0.0 copy-done
  593.9 0.0 copy-done.1
  593.9 0.0 copy-done.2
  593.9 7.3 convolution_convert_fusion
  601.2 6.4 copy.25
  607.6 57.6 %all_to_all.70 = bf16[256,64,128]{2,1,0:T(8,128)(2,1)S(1)} all-to-all(bf16[256,64,128]{2,1,0:T(8,128)(2,1)} %copy.25), channel_id=1, replica_groups=mesh['row'=8,'col'=16] {'col'}, dimensions={0} | all-to-all | bytes 8388608 | tf_op jit(solution)/shard_map/all_to_all | solution.py:109
  665.3 1.4 copy.26
  666.6 20.5 %convert_bitcast_fusion = bf16[16,1024,128]{2,1,0:T(8,128)(2,1)S(1)} fusion(bf16[16,1024,128]{2,1,0:T(8,128)(2,1)S(1)} %bitcast.75), kind=kOutput, calls=%fused_computation.28 | convolution fusion | flops 4314890240 | bytes 8388608 | tf_op jit(solution)/shard_map/zmk,my->zyk/dot_general | solution.py:110
  687.2 2.7 copy.28
  689.9 51.2 %all_to_all.71 = bf16[16,1024,128]{2,0,1:T(8,128)(2,1)S(1)} all-to-all(bf16[16,1024,128]{2,0,1:T(8,128)(2,1)S(1)} %copy.28), channel_id=1, replica_groups=mesh['row'=8,'col'=16] {'row'}, dimensions={1} | all-to-all | bytes 8388608 | tf_op jit(solution)/shard_map/all_to_all | solution.py:113
  741.0 4.7 copy.42
  745.7 7.3 all_to_all.64
  753.1 23.5 %fusion.26 = f32[16,128,1024]{2,1,0:T(8,128)} fusion(bf16[16,128,1024]{2,1,0:T(8,128)(2,1)} %all_to_all.64), kind=kOutput, calls=%fused_computation.39 | convolution fusion | flops 4312793088 | bytes 12582912 | tf_op jit(solution)/shard_map/dot_general | solution.py:114
  (4 shorter events, 0.0 us)
Async XLA Ops:
  0.0 593.9 %copy-start = (bf16[256,256]{1,0:T(8,128)(2,1)S(1)}, bf16[256,256]{1,0:T(8,128)(2,1)}, u32[]{:S(2)}) copy-start(bf16[256,256]{1,0:T(8,128)(2,1)} %param.13) | copy-start | bytes 393220
  360.5 6.4 collective-permute-start
  363.1 3.9 collective-permute-start.1
  368.2 9.8 %collective-permute-start.2 = (f32[1,130,1024]{2,1,0:T(8,128)S(1)}, f32[1,130,1024]{2,1,0:T(8,128)S(1)}, u32[]{:S(2)}, u32[]{:S(2)}) collective-permute-start(f32[1,130,1024]{2,1,0:T(8,128)S(1)} %get-tuple-element.5), channel_id=1, source_target_pairs={{0,1},{1,2},{2,3},{3,4},{4,5},{5,6},{6,7},{7,8},{8,9},{9,10},{10,1... | collective-permute-start | bytes 1597448 | tf_op jit(solution)/shard_map/ppermute | solution.py:18
  371.6 9.3 %collective-permute-start.3 = (f32[1,130,1024]{2,1,0:T(8,128)S(1)}, f32[1,130,1024]{2,1,0:T(8,128)S(1)}, u32[]{:S(2)}, u32[]{:S(2)}) collective-permute-start(f32[1,130,1024]{2,1,0:T(8,128)S(1)} %get-tuple-element.6), channel_id=1, source_target_pairs={{1,0},{2,1},{3,2},{4,3},{5,4},{6,5},{7,6},{8,7},{9,8},{10,9},{11,1... | collective-permute-start | bytes 1597448 | tf_op jit(solution)/shard_map/ppermute | solution.py:19
  522.4 66.1 %all-to-all-start.1 = ((bf16[16,1024,128]{2,0,1:T(8,128)(2,1)}), bf16[16,1024,128]{2,0,1:T(8,128)(2,1)}, u32[]{:S(2)}, u32[]{:S(2)}) async-start(bf16[16,1024,128]{2,0,1:T(8,128)(2,1)} %copy.23), calls=%async_computation.1 | async-start | bytes 8388608 | tf_op jit(solution)/shard_map/all_to_all | solution.py:85
  588.6 5.3 copy-start.1
  588.6 5.3 copy-start.2
where the time goes:
time: 787 us; the launch traced here: 777 us
  other arithmetic  364 us (46%)
  blocking collectives  161 us (20%)
  matrix products  104 us (13%)
  waiting for transfers between devices  66.6 us (8%)
  local copies, waits for them, and re-layouts  62.1 us (8%)
  starting transfers between devices  18.4 us (2%)
    scatter-add x1, other arithmetic, body(): jax.ops.segment_sum(jnp.where(live, particle_condensation_energy, 0.0), f...  345 us
    all_to_all x1, blocking collectives, body(): lax.all_to_all(levels, 'col', split_axis=0, concat_axis=1, tiled=True)  57.6 us
    all_to_all x1, waiting for transfers between devices, body(): lax.all_to_all(spectrum, 'col', split_axis=1, concat_axis=0, tiled=True)  55.7 us
    all_to_all x1, blocking collectives, body(): lax.all_to_all(along_x, 'row', split_axis=2, concat_axis=1, tiled=True)  52 us
    all_to_all x1, blocking collectives, body(): lax.all_to_all(back_y, 'row', split_axis=1, concat_axis=2, tiled=True)  51.2 us
    dot_general x1, matrix products, body(): jnp.dot(thermal_source_term, table_x, preferred_element_type=jnp.float32)  29.7 us
    dot_general x1, matrix products, body(): return jnp.dot(pencil_home, table_x, preferred_element_type=jnp.float32)  23.5 us
    dot_general x1, matrix products, body(): jnp.einsum('zyk,ym->zmk', gathered_y, table_y, preferred_element_type=jnp...  23.3 us
  transfers between devices with their start and end apart: 5, of which 4 were waited for; matrix products, arithmetic and copies ran while one was open for 0% of the time, Pallas kernels for 0%

commit v1 on v0

v1 whole, which is shorter than its diff:
```python
import functools
import math

import jax
import jax.numpy as jnp
import ml_dtypes
import numpy as np
from jax import lax
from jax.experimental import pallas as pl
from jax.experimental.pallas import tpu as pltpu
from jax.sharding import PartitionSpec as P

DIFFUSION = 0.1
MESH = pl.DeviceIdType.MESH
F32 = jnp.float32
BF16 = jnp.bfloat16
ROWS, COLS = 8, 16
DEVICES = ROWS * COLS
NX = NY = 1024
NZ = 256
CY, CZ = 128, 16
OWN = NX // DEVICES
PARTS = 4
QUAD = CZ // PARTS
MSG = QUAD * OWN
PHASES = 4
PAIR = OWN // PHASES
ORDER = (1, 2, 0, 3)
LANES = 128


def cas_table(length):
    index = np.arange(length)
    angle = (index[:, None] * index[None, :] % length) * (2.0 * math.pi / length)
    return ((np.cos(angle) + np.sin(angle)) / math.sqrt(length)).astype(ml_dtypes.bfloat16)


def dot(a, b, contract):
    return lax.dot_general(a, b, (contract, ((), ())), preferred_element_type=F32)


def partner(row, col, i):
    j = lax.rem(i * 37, DEVICES)
    x, z_lo = row // 2, lax.rem(row, 2)
    z_hi, y, core = col // 8, lax.rem(col // 2, 4), lax.rem(col, 2)
    x = lax.rem(x + j // 32, 4)
    y = lax.rem(y + lax.rem(j // 8, 4), 4)
    z = lax.rem(z_hi * 2 + z_lo + lax.rem(j // 2, 4), 4)
    core = lax.rem(core + lax.rem(j, 2), 2)
    return x * 2 + lax.rem(z, 2), (z // 2) * 8 + y * 2 + core


def spectral_kernel(
    deposit, thermal, table, analysis, synthesis, damping, wave_y,
    home,
    padded, field, forcing, outgoing, incoming, lines, solved, modes,
    edge_lo, edge_hi, halo_lo, halo_hi, corners, plane_out, plane_in,
    load_sems, edge_send, edge_recv, send_sems, recv_sems, own_sems, back_send, back_recv, back_own,
):
    row, col = lax.axis_index("row"), lax.axis_index("col")
    me = row * COLS + col
    barrier = pltpu.get_barrier_semaphore()

    def greet(i, carry):
        r, c = partner(row, col, i)
        pl.semaphore_signal(barrier, inc=1, device_id=(r, c), device_id_type=MESH)
        return carry

    deposit_load = pltpu.make_async_copy(
        deposit, padded.at[pl.ds(1, CZ), pl.ds(8, CY), :], load_sems.at[0]
    )
    deposit_load.start()
    field_load = pltpu.make_async_copy(thermal, field, load_sems.at[1])
    field_load.start()
    lax.fori_loop(1, DEVICES, greet, 0)
    deposit_load.wait()

    for z in range(CZ):
        edge_lo[z : z + 1, :] = padded[1 + z, 8:9, :]
        edge_hi[z : z + 1, :] = padded[1 + z, 7 + CY : 8 + CY, :]
    plane_out[0] = padded[1, 8 : 8 + CY, :].astype(BF16)
    plane_out[1] = padded[CZ, 8 : 8 + CY, :].astype(BF16)
    pl.semaphore_wait(barrier, DEVICES - 1)
    row_up, row_dn = lax.rem(row + 1, ROWS), lax.rem(row + ROWS - 1, ROWS)
    col_up, col_dn = lax.rem(col + 1, COLS), lax.rem(col + COLS - 1, COLS)
    top, low = pl.ds(CZ - 8, 8), pl.ds(0, 8)
    halo_copies = []
    for n, (src, dst, where) in enumerate((
        (edge_hi, halo_lo, (row_up, col)),
        (edge_lo, halo_hi, (row_dn, col)),
        (edge_hi.at[top], corners.at[0], (row_up, col_up)),
        (edge_lo.at[top], corners.at[1], (row_dn, col_up)),
        (edge_hi.at[low], corners.at[2], (row_up, col_dn)),
        (edge_lo.at[low], corners.at[3], (row_dn, col_dn)),
        (plane_out.at[1], plane_in.at[0], (row, col_up)),
        (plane_out.at[0], plane_in.at[1], (row, col_dn)),
    )):
        copy = pltpu.make_async_remote_copy(
            src, dst, edge_send.at[n], edge_recv.at[n], device_id=where, device_id_type=MESH
        )
        copy.start()
        halo_copies.append(copy)
    for n in (0, 1):
        halo_copies[n].wait_recv()
    for z in range(CZ):
        padded[1 + z, 7:8, :] = halo_lo[z : z + 1, :]
        padded[1 + z, 8 + CY : 9 + CY, :] = halo_hi[z : z + 1, :]
    field_load.wait()

    def smooth(part):
        def block(n, carry):
            level = part * QUAD + n // 4
            start = pl.multiple_of(lax.rem(n, 4) * 32, 32)
            window = pl.ds(start, 48)
            mixed = 0.5 * padded[level + 1, window, :] + 0.25 * (
                padded[level, window, :] + padded[level + 2, window, :]
            )
            mixed = 0.5 * mixed[8:40] + 0.25 * (mixed[7:39] + mixed[9:41])
            mixed = 0.5 * mixed + 0.25 * (pltpu.roll(mixed, 1, 1) + pltpu.roll(mixed, NX - 1, 1))
            total = field[level, pl.ds(start, 32), :] + mixed
            forcing[pl.ds(pl.multiple_of(n * 32, 32), 32), :] = total.astype(BF16)
            return carry

        lax.fori_loop(0, 4 * QUAD, block, 0)

    def along_x(part):
        def block(n, carry):
            k = pl.multiple_of(n * 256, 256)
            out = dot(table[pl.ds(k, 256), :], forcing[...], ((1,), (1,)))
            for pair in range(QUAD // 2):
                both = [
                    out[:, z * CY : (z + 1) * CY].reshape(32, OWN, CY)
                    for z in (2 * pair, 2 * pair + 1)
                ]
                outgoing[part, pl.ds(n * 32, 32), pair * 16 : pair * 16 + 16, :] = jnp.concatenate(
                    both, axis=1
                ).astype(BF16)
            return carry

        lax.fori_loop(0, NX // 256, block, 0)

    def landing(part):
        return incoming.at[
            part,
            pl.ds(pl.multiple_of(col * MSG, MSG), MSG),
            pl.ds(pl.multiple_of(row * CY, CY), CY),
        ]

    def send(part):
        def one(i, carry):
            r, c = partner(row, col, i)
            pltpu.make_async_remote_copy(
                outgoing.at[part, r * COLS + c], landing(part), send_sems.at[part], recv_sems.at[part],
                device_id=(r, c), device_id_type=MESH,
            ).start()
            return carry

        lax.fori_loop(1, DEVICES, one, 0)
        own = pltpu.make_async_copy(outgoing.at[part, me], landing(part), own_sems.at[part])
        own.start()
        return own

    owns = {}
    for part in ORDER:
        if part == ORDER[2]:
            for copy in halo_copies[2:]:
                copy.wait_recv()
            below, above = plane_in[0].astype(F32), plane_in[1].astype(F32)
            has_below, has_above = col > 0, col < COLS - 1
            padded[0, 8 : 8 + CY, :] = jnp.where(has_below, below, 0.0)
            padded[CZ + 1, 8 : 8 + CY, :] = jnp.where(has_above, above, 0.0)
            padded[0, 7:8, :] = jnp.where(has_below, corners[0, 7:8, :], 0.0)
            padded[0, 8 + CY : 9 + CY, :] = jnp.where(has_below, corners[1, 7:8, :], 0.0)
            padded[CZ + 1, 7:8, :] = jnp.where(has_above, corners[2, 0:1, :], 0.0)
            padded[CZ + 1, 8 + CY : 9 + CY, :] = jnp.where(has_above, corners[3, 0:1, :], 0.0)
        smooth(part)
        along_x(part)
        owns[part] = send(part)

    for part in ORDER:
        owns[part].wait()
        arrived = outgoing.at[part, pl.ds(0, DEVICES - 1)]
        pltpu.make_async_copy(arrived, arrived, recv_sems.at[part]).wait()

        def along_y(n, carry, part=part):
            rows = pl.ds(pl.multiple_of(n * 128, 128), 128)
            out = dot(incoming[part, rows, :], table[...], ((1,), (0,)))
            for tile in range(NY // LANES):
                lines[part, tile, rows, :] = out[:, tile * LANES : (tile + 1) * LANES]
            return carry

        lax.fori_loop(0, COLS * MSG // 128, along_y, 0)

    def solve(k, carry):
        wave = me * OWN + k
        folded = jnp.minimum(wave, NX - wave).astype(F32) * (2.0 * math.pi / NX)
        base = 1.0 + DIFFUSION * folded * folded

        def strip(n, c):
            m = pl.ds(pl.multiple_of(n * 256, 256), 256)
            every = pl.ds(k, COLS * QUAD, stride=OWN)
            planes = jnp.concatenate(
                [
                    jnp.concatenate([lines[part, 2 * n + t, every, :] for t in range(2)], axis=1)
                    for part in range(PARTS)
                ],
                axis=0,
            ).astype(BF16)
            modal = dot(analysis[...], planes, ((1,), (0,)))
            denom = (base + DIFFUSION * wave_y[0:1, m]) + damping[...]
            scaled = (modal / denom).astype(BF16)
            modes[:, m] = dot(synthesis[...], scaled, ((1,), (0,))).astype(BF16)
            return c

        lax.fori_loop(0, NY // 256, strip, 0)

        def back(n, c):
            rows = pl.ds(pl.multiple_of(n * 128, 128), 128)
            solved[k, rows, :] = dot(modes[rows, :], table[...], ((1,), (0,))).astype(BF16)
            return c

        lax.fori_loop(0, NZ // 128, back, 0)
        return carry

    def piece(phase, r, c):
        return solved.at[
            pl.ds(phase * PAIR, PAIR),
            pl.ds(pl.multiple_of(c * CZ, CZ), CZ),
            pl.ds(pl.multiple_of(r * CY, CY), CY),
        ]

    back_owns = []
    for phase in range(PHASES):
        lax.fori_loop(phase * PAIR, (phase + 1) * PAIR, solve, 0)
        place = home.at[pl.ds(me * OWN + phase * PAIR, PAIR)]

        def give(i, carry, phase=phase, place=place):
            r, c = partner(row, col, i)
            pltpu.make_async_remote_copy(
                piece(phase, r, c), place, back_send, back_recv, device_id=(r, c), device_id_type=MESH
            ).start()
            return carry

        lax.fori_loop(1, DEVICES, give, 0)
        own = pltpu.make_async_copy(piece(phase, row, col), place, back_own.at[phase])
        own.start()
        back_owns.append(own)

    for own in back_owns:
        own.wait()
    everything = home.at[pl.ds(0, NX - OWN)]
    pltpu.make_async_copy(everything, everything, back_recv).wait()
    pltpu.make_async_copy(everything, everything, back_send).wait()
    for part in range(PARTS):
        sent = outgoing.at[part, pl.ds(0, DEVICES - 1)]
        pltpu.make_async_copy(sent, sent, send_sems.at[part]).wait()
    for copy in halo_copies:
        copy.wait_send()


def spectral_step(deposit, thermal, table, analysis, synthesis, damping, wave_y):
    any_space, vmem = pl.BlockSpec(memory_space=pl.ANY), pl.BlockSpec(memory_space=pltpu.VMEM)
    return pl.pallas_call(
        spectral_kernel,
        out_shape=jax.ShapeDtypeStruct((NX, CZ, CY), BF16),
        in_specs=[any_space, any_space, vmem, vmem, vmem, vmem, vmem],
        out_specs=any_space,
        scratch_shapes=[
            pltpu.VMEM((CZ + 2, CY + 16, NX), F32),
            pltpu.VMEM((CZ, CY, NX), F32),
            pltpu.VMEM((QUAD * CY, NX), BF16),
            pltpu.VMEM((PARTS, DEVICES, MSG, CY), BF16),
            pltpu.VMEM((PARTS, COLS * MSG, NY), BF16),
            pltpu.VMEM((PARTS, NY // LANES, COLS * MSG, LANES), F32),
            pltpu.VMEM((OWN, NZ, NY), BF16),
            pltpu.VMEM((NZ, NY), BF16),
            pltpu.VMEM((CZ, NX), F32),
            pltpu.VMEM((CZ, NX), F32),
            pltpu.VMEM((CZ, NX), F32),
            pltpu.VMEM((CZ, NX), F32),
            pltpu.VMEM((4, 8, NX), F32),
            pltpu.VMEM((2, CY, NX), BF16),
            pltpu.VMEM((2, CY, NX), BF16),
            pltpu.SemaphoreType.DMA((2,)),
            pltpu.SemaphoreType.DMA((8,)),
            pltpu.SemaphoreType.DMA((8,)),
            pltpu.SemaphoreType.DMA((PARTS,)),
            pltpu.SemaphoreType.DMA((PARTS,)),
            pltpu.SemaphoreType.DMA((PARTS,)),
            pltpu.SemaphoreType.DMA,
            pltpu.SemaphoreType.DMA,
            pltpu.SemaphoreType.DMA((PHASES,)),
        ],
        compiler_params=pltpu.CompilerParams(
            collective_id=0, has_side_effects=True, vmem_limit_bytes=60 * 2**20
        ),
        name="spectral_step",
    )(deposit, thermal, table, analysis, synthesis, damping, wave_y)


def home_kernel(home, table, out, rows):
    @pl.when(pl.program_id(0) == 0)
    def _():
        def widen(n, carry):
            k = pl.multiple_of(n * 32, 32)
            rows[pl.ds(pl.multiple_of(n * 32 * CZ, 512), 32 * CZ), :] = (
                home[pl.ds(k, 32)].astype(F32).reshape(32 * CZ, CY)
            )
            return carry

        lax.fori_loop(0, NX // 32, widen, 0)

    level = pl.program_id(0) * 2
    both = jnp.concatenate(
        [rows[pl.ds(level + z, NX, stride=CZ), :].astype(BF16) for z in range(2)], axis=1
    )
    for x in range(0, NX, 256):
        part = dot(both, table[:, x : x + 256], ((0,), (0,)))
        out[:, :, x : x + 256] = part.reshape(2, CY, 256)


def home_step(home, table):
    return pl.pallas_call(
        home_kernel,
        grid=(CZ // 2,),
        out_shape=jax.ShapeDtypeStruct((CZ, CY, NX), F32),
        in_specs=[
            pl.BlockSpec((NX, CZ, CY), lambda i: (0, 0, 0)),
            pl.BlockSpec((NX, NX), lambda i: (0, 0)),
        ],
        out_specs=pl.BlockSpec((2, CY, NX), lambda i: (i, 0, 0)),
        scratch_shapes=[pltpu.VMEM((NX * CZ, CY), F32)],
        compiler_params=pltpu.CompilerParams(vmem_limit_bytes=50 * 2**20),
        name="home_step",
    )(home, table)


def scatter(location, energy, tally):
    live = jnp.arange(energy.shape[0], dtype=jnp.int32) < tally[0]
    flat = (location[2] * CY + location[1]) * NX + location[0]
    return jax.ops.segment_sum(
        jnp.where(live, energy, 0.0), flat, num_segments=CZ * CY * NX
    ).reshape(CZ, CY, NX)


def body(thermal, location, energy, tally, decay, analysis, synthesis):
    deposit = scatter(location, energy, tally)
    table = jnp.asarray(cas_table(NX))
    analysis = analysis.reshape(NZ, COLS, PARTS, QUAD).transpose(0, 2, 1, 3).reshape(NZ, NZ)
    index = np.arange(NY)
    wave_y = ((np.minimum(index, NY - index) * (2.0 * math.pi / NY)) ** 2).astype(np.float32)
    home = spectral_step(
        deposit, thermal, table, analysis, synthesis, decay[:, None], jnp.asarray(wave_y)[None, :]
    )
    return home_step(home, table)


def solution(mesh):
    in_specs = (
        P("col", "row", None),
        P(None, ("row", "col")),
        P(("row", "col")),
        P(("row", "col")),
        P(),
        P(),
        P(),
    )
    return jax.shard_map(
        body, mesh=mesh, in_specs=in_specs, out_specs=P("col", "row", None), check_vma=False
    )
```

time: 787 us -> 512 us (0.65); the launches traced: 777 us -> 511 us
  blocking collectives: 161 us -> 0 us
  Pallas kernels: 0 us -> 150 us
  matrix products: 104 us -> 0 us
  waiting for transfers between devices: 66.6 us -> 0 us
  local copies, waits for them, and re-layouts: 62.1 us -> 11.1 us
  starting transfers between devices: 18.4 us -> 0 us
  other arithmetic: 364 us -> 349 us
    all_to_all x3 -> x0, blocking collectives: 161 us -> none  [the longest x1 57.6 us: body(): lax.all_to_all(levels, 'col', split_axis=0, concat_axis=1, tiled=True)]
    pallas_call x0 -> x2, Pallas kernels: none -> 150 us  [the longest x1 137 us: spectral_step(): pl.pallas_call(spectral_kernel, out_shape=jax.ShapeDtypeStruct((NX, CZ, C...]
    dot_general x5 -> x0, matrix products: 104 us -> none  [the longest x1 29.7 us: body(): jnp.dot(thermal_source_term, table_x, preferred_element_type=jnp.float32)]
    all_to_all x1 -> x0, waiting for transfers between devices: 55.7 us -> none  [body(): lax.all_to_all(spectrum, 'col', split_axis=1, concat_axis=0, tiled=True)]
    all_to_all x5 -> x0, local copies, waits for them, and re-layouts: 25.3 us -> none  [the longest x2 12 us: body(): lax.all_to_all(back_y, 'row', split_axis=1, concat_axis=2, tiled=True)]
    convert_element_type x3 -> x0, local copies, waits for them, and re-layouts: 14.2 us -> none  [the longest x1 6.8 us: body(): jnp.dot(thermal_source_term, table_x, preferred_element_type=jnp.float32)]
    ppermute x4 -> x0, waiting for transfers between devices: 10.8 us -> none  [the longest x2 8.04 us: with_halo(): before = lax.ppermute(last, axis, up)]
    all_to_all x1 -> x0, starting transfers between devices: 10.2 us -> none  [body(): lax.all_to_all(spectrum, 'col', split_axis=1, concat_axis=0, tiled=True)]
  transfers between devices with their start and end apart: 5 -> 0, of which waited for: 4 -> 0; matrix products, arithmetic and copies ran while one was open for 0% -> 0% of each run, Pallas kernels for 0% -> 0%
where the time goes in v1:
time: 512 us; the launch traced here: 511 us
  other arithmetic  349 us (68%)
  Pallas kernels  150 us (29%)
  local copies, waits for them, and re-layouts  11.1 us (2%)
    scatter-add x1, other arithmetic, scatter(): jax.ops.segment_sum(jnp.where(live, energy, 0.0), flat, num_segments=CZ *...  345 us
    pallas_call x1, Pallas kernels, spectral_step(): pl.pallas_call(spectral_kernel, out_shape=jax.ShapeDtypeStruct((NX, CZ, C...  137 us
    pallas_call x1, Pallas kernels, home_step(): pl.pallas_call(home_kernel, grid=(CZ // 2,), out_shape=jax.ShapeDtypeStru...  13.1 us

profile of v1, /device:TPU:1, one launch (start us, length us, event | category | flops | bytes accessed | tf_op | source)
XLA Modules:
  0.0 511.2 jit_solution(15424482897900141859)
XLA Ops:
  0.7 1.0 fusion.2
  1.6 2.9 slice_add_fusion
  4.5 345.4 %scatter_custom_fusion = f32[2097152]{0:T(1024)} fusion(s32[65536]{0:T(1024)S(1)} %bitcast.10, f32[65536]{0:T(1024)S(1)} %fusion.2, f32[]{:T(128)} %constant.5.clone.1), kind=kCustom, calls=%fused_computation.1 | custom fusion | flops 65536 | bytes 8388612 | tf_op jit(solution)/shard_map/scatter-add | solution.py:341
  349.9 0.0 copy-start.1
  349.9 0.0 copy-start.2
  349.9 9.3 %reshape.48.deposit = f32[16,128,1024]{2,1,0:T(8,128)} reshape(f32[2097152]{0:T(1024)} %scatter_custom_fusion) | data formatting | bytes 16777216 | tf_op jit(solution)/shard_map/reshape | solution.py:343
  359.2 0.0 copy-done.1
  359.2 0.1 copy.11
  359.5 0.8 copy.13.analysis
  360.2 0.0 copy-done.2
  360.2 0.8 copy.14.damping
  361.0 0.0 copy-start
  361.0 137.1 %spectral_step.1.home = bf16[1024,16,128]{2,1,0:T(8,128)(2,1)} custom-call(f32[16,128,1024]{2,1,0:T(8,128)} %reshape.48.deposit, f32[16,128,1024]{2,1,0:T(8,128)} %thermal.1, bf16[1024,1024]{1,0:T(8,128)(2,1)} %constant.4.clone.table, bf16[256,256]{1,0:T(8,128)(2,1)} %copy.13.analysis, bf16[256,256]{1,0:T(8,128)(2,1)} %synthesis.1, f32[256,1]{1,0:T(8,128)} %copy.14.damping, ...), custom_call_target="tpu_custom_call" | custom-call | tf_op jit(solution)/shard_map/spectral_step/pallas_call | solution.py:263
  498.1 0.0 copy-done
  498.1 13.1 %home_step.1 = f32[16,128,1024]{2,1,0:T(8,128)} custom-call(bf16[1024,16,128]{2,1,0:T(8,128)(2,1)} %spectral_step.1.home, bf16[1024,1024]{1,0:T(8,128)(2,1)S(1)} %copy-done), custom_call_target="tpu_custom_call" | custom-call | tf_op jit(solution)/shard_map/home_step/pallas_call | solution.py:323
  (3 shorter events, 0.1 us)
Async XLA Ops:
  349.9 9.3 %copy-start.1 = (bf16[256,256]{1,0:T(8,128)(2,1)S(1)}, bf16[256,256]{1,0:T(8,128)(2,1)}, u32[]{:S(2)}) copy-start(bf16[256,256]{1,0:T(8,128)(2,1)} %param.14) | copy-start | bytes 393220
  349.9 10.3 %copy-start.2 = (f32[256]{0:T(256)S(1)}, f32[256]{0:T(256)}, u32[]{:S(2)}) copy-start(f32[256]{0:T(256)} %param.13) | copy-start | bytes 3076
  361.0 137.1 %copy-start = (bf16[1024,1024]{1,0:T(8,128)(2,1)S(1)}, bf16[1024,1024]{1,0:T(8,128)(2,1)}, u32[]{:S(2)}) copy-start(bf16[1024,1024]{1,0:T(8,128)(2,1)} %constant.4.clone.table) | copy-start | bytes 6291460

commit v2 on v1

v2 whole, which is shorter than its diff:
```python
import functools
import math

import jax
import jax.numpy as jnp
import ml_dtypes
import numpy as np
from jax import lax
from jax.experimental import pallas as pl
from jax.experimental.pallas import tpu as pltpu
from jax.sharding import PartitionSpec as P

DIFFUSION = 0.1
MESH = pl.DeviceIdType.MESH
F32 = jnp.float32
BF16 = jnp.bfloat16
ROWS, COLS = 8, 16
DEVICES = ROWS * COLS
NX = NY = 1024
NZ = 256
CY, CZ = 128, 16
OWN = NX // DEVICES
PARTS = 4
QUAD = CZ // PARTS
MSG = QUAD * OWN
PHASES = (0, 1, 3, 5, 7, 8)
ORDER = (1, 2, 0, 3)
LANES = 128
WINDOW = 6
GROUPS = CZ * NX // LANES


def cas_table(length):
    index = np.arange(length)
    angle = (index[:, None] * index[None, :] % length) * (2.0 * math.pi / length)
    return ((np.cos(angle) + np.sin(angle)) / math.sqrt(length)).astype(ml_dtypes.bfloat16)


def dot(a, b, contract):
    return lax.dot_general(a, b, (contract, ((), ())), preferred_element_type=F32)


def for_partners(row, col, act):
    x, y, z, core = row >> 1, (col >> 1) & 3, ((col >> 3) << 1) + (row & 1), col & 1
    depths = [(z + t) & 3 for t in range(4)]
    z_row = [depth & 1 for depth in depths]
    z_col = [((depth >> 1) << 3) + c for depth in depths for c in (core, core ^ 1)]

    def group(x, y, skip):
        for t in range(4):
            r = (((x + t) & 3) << 1) + z_row[t]
            near = ((y + t) & 3) << 1
            for c in range(2):
                if t or c or not skip:
                    act(r, z_col[2 * t + c] + near)

    def step(i, carry):
        group(x + (i >> 2), y + (i & 3), False)
        return carry

    group(x, y, True)
    lax.fori_loop(1, DEVICES // 8, step, 0)


def spectral_kernel(
    deposit, thermal, table, analysis, synthesis, damping, wave_y,
    home,
    padded, field, forcing, outgoing, incoming, lines, solved, modes,
    arrivals, wide, turned, edge_lo, edge_hi, halo_lo, halo_hi, corners, plane_out, plane_in,
    load_sems, edge_send, edge_recv, send_sems, recv_sems, own_sems, back_send, back_recv, back_own, home_sems,
):
    row, col = lax.axis_index("row"), lax.axis_index("col")
    me = row * COLS + col
    barrier = pltpu.get_barrier_semaphore()

    def greet(r, c):
        pl.semaphore_signal(barrier, inc=1, device_id=(r, c), device_id_type=MESH)

    deposit_load = pltpu.make_async_copy(
        deposit, padded.at[pl.ds(1, CZ), pl.ds(8, CY), :], load_sems.at[0]
    )
    deposit_load.start()
    field_load = pltpu.make_async_copy(thermal, field, load_sems.at[1])
    field_load.start()
    for_partners(row, col, greet)
    deposit_load.wait()

    def smooth(levels, blocks):
        low, count = levels[0], len(blocks)
        step, stride = levels[1] - levels[0], blocks[1] - blocks[0]

        def block(n, carry):
            level = low + n // count * step
            start = pl.multiple_of((blocks[0] + n % count * stride) * 16, 16)
            window = pl.ds(start, 32)
            mixed = 0.5 * padded[level + 1, window, :] + 0.25 * (
                padded[level, window, :] + padded[level + 2, window, :]
            )
            mixed = 0.5 * mixed[8:24] + 0.25 * (mixed[7:23] + mixed[9:25])
            mixed = 0.5 * mixed + 0.25 * (pltpu.roll(mixed, 1, 1) + pltpu.roll(mixed, NX - 1, 1))
            total = field[level, pl.ds(start, 16), :] + mixed
            forcing[pl.ds(pl.multiple_of(level * CY + start, 16), 16), :] = total.astype(BF16)
            return carry

        lax.fori_loop(0, len(levels) * count, block, 0)

    inner, outer = range(1, CY // 16 - 1), (0, CY // 16 - 1)

    for z in range(CZ):
        edge_lo[z : z + 1, :] = padded[1 + z, 8:9, :]
        edge_hi[z : z + 1, :] = padded[1 + z, 7 + CY : 8 + CY, :]
    plane_out[0] = padded[1, 8 : 8 + CY, :].astype(BF16)
    plane_out[1] = padded[CZ, 8 : 8 + CY, :].astype(BF16)
    field_load.wait()
    smooth(range(QUAD, CZ - QUAD), inner)
    pl.semaphore_wait(barrier, DEVICES - 1)
    row_up, row_dn = lax.rem(row + 1, ROWS), lax.rem(row + ROWS - 1, ROWS)
    col_up, col_dn = lax.rem(col + 1, COLS), lax.rem(col + COLS - 1, COLS)
    top, low = pl.ds(CZ - 8, 8), pl.ds(0, 8)
    halo_copies = []
    for n, (src, dst, where) in enumerate((
        (edge_hi, halo_lo, (row_up, col)),
        (edge_lo, halo_hi, (row_dn, col)),
        (edge_hi.at[top], corners.at[0], (row_up, col_up)),
        (edge_lo.at[top], corners.at[1], (row_dn, col_up)),
        (edge_hi.at[low], corners.at[2], (row_up, col_dn)),
        (edge_lo.at[low], corners.at[3], (row_dn, col_dn)),
        (plane_out.at[1], plane_in.at[0], (row, col_up)),
        (plane_out.at[0], plane_in.at[1], (row, col_dn)),
    )):
        copy = pltpu.make_async_remote_copy(
            src, dst, edge_send.at[n], edge_recv.at[n], device_id=where, device_id_type=MESH
        )
        copy.start()
        halo_copies.append(copy)
    smooth(range(1, QUAD), inner)
    smooth(range(CZ - QUAD, CZ - 1), inner)
    for n in (0, 1):
        halo_copies[n].wait_recv()
    for z in range(CZ):
        padded[1 + z, 7:8, :] = halo_lo[z : z + 1, :]
        padded[1 + z, 8 + CY : 9 + CY, :] = halo_hi[z : z + 1, :]

    def along_x(part):
        def block(n, carry):
            k = pl.multiple_of(n * 512, 512)
            out = dot(
                table[pl.ds(k, 512), :], forcing[part * QUAD * CY : (part + 1) * QUAD * CY, :], ((1,), (1,))
            )
            for pair in range(QUAD // 2):
                both = [
                    out[:, z * CY : (z + 1) * CY].reshape(64, OWN, CY)
                    for z in (2 * pair, 2 * pair + 1)
                ]
                outgoing[part, pl.ds(n * 64, 64), pair * 16 : pair * 16 + 16, :] = jnp.concatenate(
                    both, axis=1
                ).astype(BF16)
            return carry

        lax.fori_loop(0, NX // 512, block, 0)

    def landing(part):
        return incoming.at[
            part,
            pl.ds(pl.multiple_of(col * MSG, MSG), MSG),
            pl.ds(pl.multiple_of(row * CY, CY), CY),
        ]

    def send(part):
        def one(r, c):
            pltpu.make_async_remote_copy(
                outgoing.at[part, r * COLS + c], landing(part), send_sems.at[part], recv_sems.at[part],
                device_id=(r, c), device_id_type=MESH,
            ).start()

        for_partners(row, col, one)
        own = pltpu.make_async_copy(outgoing.at[part, me], landing(part), own_sems.at[part])
        own.start()
        return own

    owns = {}
    for part in ORDER:
        if part == ORDER[2]:
            for copy in halo_copies[2:]:
                copy.wait_recv()
            below, above = plane_in[0].astype(F32), plane_in[1].astype(F32)
            has_below, has_above = col > 0, col < COLS - 1
            padded[0, 8 : 8 + CY, :] = jnp.where(has_below, below, 0.0)
            padded[CZ + 1, 8 : 8 + CY, :] = jnp.where(has_above, above, 0.0)
            padded[0, 7:8, :] = jnp.where(has_below, corners[0, 7:8, :], 0.0)
            padded[0, 8 + CY : 9 + CY, :] = jnp.where(has_below, corners[1, 7:8, :], 0.0)
            padded[CZ + 1, 7:8, :] = jnp.where(has_above, corners[2, 0:1, :], 0.0)
            padded[CZ + 1, 8 + CY : 9 + CY, :] = jnp.where(has_above, corners[3, 0:1, :], 0.0)
            smooth((0, CZ - 1), inner)
            smooth((0, CZ - 1), outer)
        levels = range(part * QUAD, (part + 1) * QUAD)
        smooth([z for z in levels if 0 < z < CZ - 1], outer)
        along_x(part)
        owns[part] = send(part)

    for part in ORDER:
        owns[part].wait()
        arrived = outgoing.at[part, pl.ds(0, DEVICES - 1)]
        pltpu.make_async_copy(arrived, arrived, recv_sems.at[part]).wait()

        def along_y(n, carry, part=part):
            rows = pl.ds(pl.multiple_of(n * 512, 512), 512)
            out = dot(incoming[part, rows, :], table[...], ((1,), (0,)))
            for tile in range(NY // LANES):
                lines[part, tile, rows, :] = out[:, tile * LANES : (tile + 1) * LANES]
            return carry

        lax.fori_loop(0, COLS * MSG // 512, along_y, 0)

    def solve(k, carry):
        wave = me * OWN + k
        folded = jnp.minimum(wave, NX - wave).astype(F32) * (2.0 * math.pi / NX)
        base = 1.0 + DIFFUSION * folded * folded

        every = pl.ds(k, COLS * QUAD, stride=OWN)
        for n in range(NY // 256):
            planes = jnp.concatenate(
                [
                    jnp.concatenate([lines[part, 2 * n + t, every, :] for t in range(2)], axis=1)
                    for part in range(PARTS)
                ],
                axis=0,
            ).astype(BF16)
            modal = dot(analysis[...], planes, ((1,), (0,)))
            denom = (base + DIFFUSION * wave_y[0:1, n * 256 : (n + 1) * 256]) + damping[...]
            scaled = (modal / denom).astype(BF16)
            modes[:, n * 256 : (n + 1) * 256] = dot(synthesis[...], scaled, ((1,), (0,))).astype(BF16)
        solved[k] = dot(modes[...], table[...], ((1,), (0,))).astype(BF16)
        return carry

    def piece(begin, end, r, c):
        return solved.at[
            pl.ds(begin, end - begin),
            pl.ds(pl.multiple_of(c * CZ, CZ), CZ),
            pl.ds(pl.multiple_of(r * CY, CY), CY),
        ]

    back_owns = []
    spans = list(enumerate(zip(PHASES[:-1], PHASES[1:])))
    for phase, (begin, end) in spans:
        lax.fori_loop(begin, end, solve, 0)
        place = arrivals.at[pl.ds(begin, end - begin), me]

        def give(r, c, phase=phase, begin=begin, end=end, place=place):
            pltpu.make_async_remote_copy(
                piece(begin, end, r, c), place, back_send.at[phase], back_recv.at[phase],
                device_id=(r, c), device_id_type=MESH,
            ).start()

        for_partners(row, col, give)
        own = pltpu.make_async_copy(piece(begin, end, row, col), place, back_own.at[phase])
        own.start()
        back_owns.append(own)

    def turn(k):
        def widen(n, carry):
            rows = pl.ds(pl.multiple_of(n * 32 * CZ, 32 * CZ), 32 * CZ)
            wide[rows, :] = arrivals[k, pl.ds(n * 32, 32)].astype(F32).reshape(32 * CZ, CY)
            return carry

        lax.fori_loop(0, DEVICES // 32, widen, 0)
        for z in range(CZ):
            turned[k % 2, z] = wide[pl.ds(z, DEVICES, stride=CZ), :].T.astype(BF16)
        return pltpu.make_async_copy(
            turned.at[k % 2], home.at[:, :, pl.ds(k * DEVICES, DEVICES)], home_sems.at[k]
        )

    homes = []
    for phase, (begin, end) in spans:
        back_owns[phase].wait()
        arrived = arrivals.at[pl.ds(begin, end - begin), pl.ds(0, DEVICES - 1)]
        pltpu.make_async_copy(arrived, arrived, back_recv.at[phase]).wait()
        for k in range(begin, end):
            if k >= 2:
                homes[k - 2].wait()
            homes.append(turn(k))
            homes[k].start()
    for phase, (begin, end) in spans:
        sent = arrivals.at[pl.ds(begin, end - begin), pl.ds(0, DEVICES - 1)]
        pltpu.make_async_copy(sent, sent, back_send.at[phase]).wait()
    for copy in homes[-2:]:
        copy.wait()
    for part in range(PARTS):
        sent = outgoing.at[part, pl.ds(0, DEVICES - 1)]
        pltpu.make_async_copy(sent, sent, send_sems.at[part]).wait()
    for copy in halo_copies:
        copy.wait_send()


def spectral_step(deposit, thermal, table, analysis, synthesis, damping, wave_y):
    any_space, vmem = pl.BlockSpec(memory_space=pl.ANY), pl.BlockSpec(memory_space=pltpu.VMEM)
    return pl.pallas_call(
        spectral_kernel,
        out_shape=jax.ShapeDtypeStruct((CZ, CY, NX), BF16),
        in_specs=[any_space, any_space, vmem, vmem, vmem, vmem, vmem],
        out_specs=any_space,
        scratch_shapes=[
            pltpu.VMEM((CZ + 2, CY + 16, NX), F32),
            pltpu.VMEM((CZ, CY, NX), F32),
            pltpu.VMEM((CZ * CY, NX), BF16),
            pltpu.VMEM((PARTS, DEVICES, MSG, CY), BF16),
            pltpu.VMEM((PARTS, COLS * MSG, NY), BF16),
            pltpu.VMEM((PARTS, NY // LANES, COLS * MSG, LANES), F32),
            pltpu.VMEM((OWN, NZ, NY), BF16),
            pltpu.VMEM((NZ, NY), BF16),
            pltpu.VMEM((OWN, DEVICES, CZ, CY), BF16),
            pltpu.VMEM((DEVICES * CZ, CY), F32),
            pltpu.VMEM((2, CZ, CY, DEVICES), BF16),
            pltpu.VMEM((CZ, NX), F32),
            pltpu.VMEM((CZ, NX), F32),
            pltpu.VMEM((CZ, NX), F32),
            pltpu.VMEM((CZ, NX), F32),
            pltpu.VMEM((4, 8, NX), F32),
            pltpu.VMEM((2, CY, NX), BF16),
            pltpu.VMEM((2, CY, NX), BF16),
            pltpu.SemaphoreType.DMA((2,)),
            pltpu.SemaphoreType.DMA((8,)),
            pltpu.SemaphoreType.DMA((8,)),
            pltpu.SemaphoreType.DMA((PARTS,)),
            pltpu.SemaphoreType.DMA((PARTS,)),
            pltpu.SemaphoreType.DMA((PARTS,)),
            pltpu.SemaphoreType.DMA((len(PHASES) - 1,)),
            pltpu.SemaphoreType.DMA((len(PHASES) - 1,)),
            pltpu.SemaphoreType.DMA((len(PHASES) - 1,)),
            pltpu.SemaphoreType.DMA((OWN,)),
        ],
        compiler_params=pltpu.CompilerParams(
            collective_id=0, has_side_effects=True, vmem_limit_bytes=60 * 2**20
        ),
        name="spectral_step",
    )(deposit, thermal, table, analysis, synthesis, damping, wave_y)


def home_kernel(home, table, out):
    for x in range(0, NX, 256):
        out[:, x : x + 256] = dot(home[...], table[:, x : x + 256], ((1,), (0,)))


def home_step(home, table):
    rows = QUAD * CY
    out = pl.pallas_call(
        home_kernel,
        grid=(CZ // QUAD,),
        out_shape=jax.ShapeDtypeStruct((CZ * CY, NX), F32),
        in_specs=[
            pl.BlockSpec((rows, NX), lambda i: (i, 0)),
            pl.BlockSpec((NX, NX), lambda i: (0, 0)),
        ],
        out_specs=pl.BlockSpec((rows, NX), lambda i: (i, 0)),
        compiler_params=pltpu.CompilerParams(vmem_limit_bytes=50 * 2**20),
        name="home_step",
    )(home.reshape(CZ * CY, NX), table)
    return out.reshape(CZ, CY, NX)


def deposit_kernel(first, last, keys, energy, out, key_rows, energy_rows):
    level, rows = pl.program_id(0), keys.shape[0]

    @pl.when(level == 0)
    def _():
        key_rows[0:rows, :] = keys[...]
        energy_rows[0:rows, :] = energy[...]
        key_rows[rows:, :] = jnp.full((WINDOW, LANES), GROUPS * CY * LANES, jnp.int32)
        energy_rows[rows:, :] = jnp.zeros((WINDOW, LANES), F32)

    lane = lax.broadcasted_iota(jnp.int32, (LANES, LANES), 0).astype(BF16)
    one, nil = jnp.ones((LANES, LANES), BF16), jnp.zeros((LANES, LANES), BF16)

    def tile(group, start):
        chosen, high, rest = [], [], []
        for n in range(WINDOW):
            key, heat = key_rows[pl.ds(start + n, 1), :], energy_rows[pl.ds(start + n, 1), :]
            hit = lane == (key & (LANES - 1)).astype(F32).astype(BF16)
            top = heat.astype(BF16)
            high.append(jnp.where(hit, top, nil))
            rest.append(jnp.where(hit, (heat - top.astype(F32)).astype(BF16), nil))
            line = (key >> 7) - group * CY
            line = jnp.where((line >= 0) & (line < CY), line, -1).astype(F32).astype(BF16)
            chosen.append(jnp.where(lane == line, one, nil))
        weights = jnp.concatenate(
            [jnp.concatenate(high, axis=1), jnp.concatenate(rest, axis=1)], axis=0
        )
        sums = dot(jnp.concatenate(chosen, axis=1), weights, ((1,), (1,)))
        return sums[:, :LANES] + sums[:, LANES:]

    per_level = NX // LANES
    starts = [first[level * per_level + n] for n in range(per_level)]
    for n, start in enumerate(starts):
        out[0, :, n * LANES : (n + 1) * LANES] = tile(level * per_level + n, start)
    for n, start in enumerate(starts):
        group = level * per_level + n

        def further(w, c, n=n, group=group, start=start):
            out[0, :, n * LANES : (n + 1) * LANES] += tile(group, start + w * WINDOW)
            return c

        lax.fori_loop(1, (last[group] - start + WINDOW - 1) // WINDOW, further, 0)


def deposit_step(location, energy, tally):
    slots = energy.shape[0]
    live = jnp.arange(slots, dtype=jnp.int32) < tally[0]
    x = location[0]
    key = ((location[2] * (NX // LANES) + x // LANES) * CY + location[1]) * LANES + x % LANES
    key = jnp.where(live, key, GROUPS * CY * LANES)
    energy = jnp.where(live, energy, 0.0)
    key, energy = lax.sort((key, energy), num_keys=1, is_stable=False)
    key, energy = key.reshape(-1, LANES), energy.reshape(-1, LANES)
    group = jnp.arange(GROUPS, dtype=jnp.int32)[:, None] * (CY * LANES)
    first = jnp.sum((key[:, LANES - 1] < group).astype(jnp.int32), axis=1)
    last = jnp.sum((key[:, 0] < group + CY * LANES).astype(jnp.int32), axis=1)
    smem, vmem = pl.BlockSpec(memory_space=pltpu.SMEM), pl.BlockSpec(memory_space=pltpu.VMEM)
    return pl.pallas_call(
        deposit_kernel,
        out_shape=jax.ShapeDtypeStruct((CZ, CY, NX), F32),
        grid=(CZ,),
        in_specs=[smem, smem, vmem, vmem],
        out_specs=pl.BlockSpec((1, CY, NX), lambda z: (z, 0, 0)),
        scratch_shapes=[
            pltpu.VMEM((slots // LANES + WINDOW, LANES), jnp.int32),
            pltpu.VMEM((slots // LANES + WINDOW, LANES), F32),
        ],
        compiler_params=pltpu.CompilerParams(vmem_limit_bytes=50 * 2**20),
        name="deposit_step",
    )(first, last, key, energy)


def body(thermal, location, energy, tally, decay, analysis, synthesis):
    deposit = deposit_step(location, energy, tally)
    table = jnp.asarray(cas_table(NX))
    analysis = analysis.reshape(NZ, COLS, PARTS, QUAD).transpose(0, 2, 1, 3).reshape(NZ, NZ)
    index = np.arange(NY)
    wave_y = ((np.minimum(index, NY - index) * (2.0 * math.pi / NY)) ** 2).astype(np.float32)
    home = spectral_step(
        deposit, thermal, table, analysis, synthesis, decay[:, None], jnp.asarray(wave_y)[None, :]
    )
    ordered = cas_table(NX).reshape(DEVICES, OWN, NX).transpose(1, 0, 2).reshape(NX, NX)
    return home_step(home, jnp.asarray(ordered))


def solution(mesh):
    in_specs = (
        P("col", "row", None),
        P(None, ("row", "col")),
        P(("row", "col")),
        P(("row", "col")),
        P(),
        P(),
        P(),
    )
    return jax.shard_map(
        body, mesh=mesh, in_specs=in_specs, out_specs=P("col", "row", None), check_vma=False
    )
```

time: 512 us -> 191 us (0.37)
  other arithmetic: 349 us -> 22.7 us
  Pallas kernels: 150 us -> 164 us
  local copies, waits for them, and re-layouts: 11.1 us -> 3.63 us
    scatter-add x1 -> x0, other arithmetic: 345 us -> none  [scatter(): jax.ops.segment_sum(jnp.where(live, energy, 0.0), flat, num_segments=CZ *...]
    sort x0 -> x1, other arithmetic: none -> 18.2 us  [deposit_step(): key, energy = lax.sort((key, energy), num_keys=1, is_stable=False)]
    pallas_call x2 -> x3, Pallas kernels: 150 us -> 164 us  [the longest x1 133 us: spectral_step(): pl.pallas_call(spectral_kernel, out_shape=jax.ShapeDtypeStruct((CZ, CY, N...]
    reshape x1 -> x0, local copies, waits for them, and re-layouts: 9.31 us -> none  [scatter(): return jax.ops.segment_sum(jnp.where(live, energy, 0.0), flat, num_segmen...]
where the time goes in v2:
time: 191 us
  Pallas kernels  164 us (86%)
  other arithmetic  22.7 us (12%)
  local copies, waits for them, and re-layouts  3.63 us (2%)
    pallas_call x1, Pallas kernels, spectral_step(): pl.pallas_call(spectral_kernel, out_shape=jax.ShapeDtypeStruct((CZ, CY, N...  133 us
    pallas_call x1, Pallas kernels, deposit_step(): pl.pallas_call(deposit_kernel, out_shape=jax.ShapeDtypeStruct((CZ, CY, NX...  22.8 us
    sort x1, other arithmetic, deposit_step(): key, energy = lax.sort((key, energy), num_keys=1, is_stable=False)  18.2 us
    pallas_call x1, Pallas kernels, home_step(): pl.pallas_call(home_kernel, grid=(CZ // QUAD,), out_shape=jax.ShapeDtypeS...  8.4 us

profile of v2, /device:TPU:1, one launch (start us, length us, event | category | flops | bytes accessed | tf_op | source)
XLA Modules:
  0.0 190.9 jit_solution(11562641347676787036)
XLA Ops:
  0.7 1.5 copy.19.damping
  2.1 1.0 copy.16
  3.3 0.7 copy.18.analysis
  4.0 1.0 fusion.8
  5.0 3.0 %fusion.11 = (s32[1,65536]{1,0:T(1,128)S(1)}, s32[1,65536]{1,0:T(1,128)S(1)}, s32[1,65536]{1,0:T(1,128)S(1)}) fusion(s32[3,65536]{1,0:T(4,128)} %param.11), kind=kLoop, calls=%fused_computation.25 | loop fusion | flops 65536 | bytes 1572864 | tf_op jit(solution)/shard_map/slice | solution.py:408
  8.0 0.3 fusion.5
  8.4 18.2 %sort.15 = (s32[65536]{0:T(1024)S(1)}, f32[65536]{0:T(1024)S(1)}) sort(s32[65536]{0:T(1024)S(1)} %fusion.5, f32[65536]{0:T(1024)S(1)} %fusion.8), dimensions={0}, to_apply=%region_0.1 | sort | flops 1048576 | bytes 1048576 | tf_op jit(solution)/shard_map/sort | solution.py:412
  26.5 0.3 slice_reduce_fusion
  26.8 0.2 convert_reduce_fusion
  27.1 22.8 %deposit_step.1.deposit = f32[16,128,1024]{2,1,0:T(8,128)} custom-call(s32[128]{0:T(128)S(1)} %get-tuple-element.15.first, s32[128]{0:T(128)S(1)} %get-tuple-element.14.last, s32[512,128]{1,0:T(8,128)S(1)} %bitcast.17, f32[512,128]{1,0:T(8,128)S(1)} %bitcast.18), custom_call_target="tpu_custom_call" | custom-call | tf_op jit(solution)/shard_map/deposit_step/pallas_call | solution.py:418
  49.9 0.0 copy-start
  49.9 132.6 %spectral_step.1 = bf16[16,128,1024]{2,1,0:T(8,128)(2,1)} custom-call(f32[16,128,1024]{2,1,0:T(8,128)} %deposit_step.1.deposit, f32[16,128,1024]{2,1,0:T(8,128)} %thermal.1, bf16[1024,1024]{1,0:T(8,128)(2,1)} %constant.44.clone.table, bf16[256,256]{1,0:T(8,128)(2,1)} %copy.18.analysis, bf16[256,256]{1,0:T(8,128)(2,1)} %synthesis.1, f32[256,1]{1,0:T(8,128)} %copy.19.damping, ...), custom_call_target="tpu_custom_call" | custom-call | tf_op jit(solution)/shard_map/spectral_step/pallas_call | solution.py:297
  182.5 0.0 copy-done
  182.5 8.4 %home_step.1 = f32[2048,1024]{1,0:T(8,128)} custom-call(bf16[2048,1024]{1,0:T(8,128)(2,1)} %bitcast.19, bf16[1024,1024]{1,0:T(8,128)(2,1)S(1)} %copy-done), custom_call_target="tpu_custom_call" | custom-call | tf_op jit(solution)/shard_map/home_step/pallas_call | solution.py:346
  (5 shorter events, 0.1 us)
Async XLA Ops:
  49.9 132.6 %copy-start = (bf16[1024,1024]{1,0:T(8,128)(2,1)S(1)}, bf16[1024,1024]{1,0:T(8,128)(2,1)}, u32[]{:S(2)}) copy-start(bf16[1024,1024]{1,0:T(8,128)(2,1)} %constant.46.clone.table) | copy-start | bytes 6291460

commit v3 on v2

--- a/solution.py
+++ b/solution.py
@@ -63,8 +63,9 @@
 
 
 def spectral_kernel(
-    deposit, thermal, table, analysis, synthesis, damping, wave_y,
+    deposit, thermal, table, analysis, synthesis, decay, wave_y,
     home,
+    ordered, damping,
     padded, field, forcing, outgoing, incoming, lines, solved, modes,
     arrivals, wide, turned, edge_lo, edge_hi, halo_lo, halo_hi, corners, plane_out, plane_in,
     load_sems, edge_send, edge_recv, send_sems, recv_sems, own_sems, back_send, back_recv, back_own, home_sems,
@@ -81,8 +82,8 @@
     )
     deposit_load.start()
     field_load = pltpu.make_async_copy(thermal, field, load_sems.at[1])
+    for_partners(row, col, greet)
     field_load.start()
-    for_partners(row, col, greet)
     deposit_load.wait()
 
     def smooth(levels, blocks):
@@ -106,13 +107,17 @@
 
     inner, outer = range(1, CY // 16 - 1), (0, CY // 16 - 1)
 
+    place = lax.broadcasted_iota(jnp.int32, (NZ, NZ), 1)
+    level = ((place >> 2) & (COLS - 1)) * CZ + (place >> 6) * QUAD + (place & (QUAD - 1))
+    moved = (lax.broadcasted_iota(jnp.int32, (NZ, NZ), 0) == level).astype(F32).astype(BF16)
+    ordered[...] = dot(analysis[...], moved, ((1,), (0,))).astype(BF16)
+    damping[...] = jnp.broadcast_to(decay[...], (LANES, NZ)).T
+
     for z in range(CZ):
         edge_lo[z : z + 1, :] = padded[1 + z, 8:9, :]
         edge_hi[z : z + 1, :] = padded[1 + z, 7 + CY : 8 + CY, :]
     plane_out[0] = padded[1, 8 : 8 + CY, :].astype(BF16)
     plane_out[1] = padded[CZ, 8 : 8 + CY, :].astype(BF16)
-    field_load.wait()
-    smooth(range(QUAD, CZ - QUAD), inner)
     pl.semaphore_wait(barrier, DEVICES - 1)
     row_up, row_dn = lax.rem(row + 1, ROWS), lax.rem(row + ROWS - 1, ROWS)
     col_up, col_dn = lax.rem(col + 1, COLS), lax.rem(col + COLS - 1, COLS)
@@ -133,8 +138,8 @@
         )
         copy.start()
         halo_copies.append(copy)
-    smooth(range(1, QUAD), inner)
-    smooth(range(CZ - QUAD, CZ - 1), inner)
+    field_load.wait()
+    smooth(range(QUAD, CZ - QUAD), inner)
     for n in (0, 1):
         halo_copies[n].wait_recv()
     for z in range(CZ):
@@ -193,6 +198,8 @@
             padded[CZ + 1, 8 + CY : 9 + CY, :] = jnp.where(has_above, corners[3, 0:1, :], 0.0)
             smooth((0, CZ - 1), inner)
             smooth((0, CZ - 1), outer)
+            smooth(range(1, QUAD), inner)
+            smooth(range(CZ - QUAD, CZ - 1), inner)
         levels = range(part * QUAD, (part + 1) * QUAD)
         smooth([z for z in levels if 0 < z < CZ - 1], outer)
         along_x(part)
@@ -226,8 +233,8 @@
                 ],
                 axis=0,
             ).astype(BF16)
-            modal = dot(analysis[...], planes, ((1,), (0,)))
-            denom = (base + DIFFUSION * wave_y[0:1, n * 256 : (n + 1) * 256]) + damping[...]
+            modal = dot(ordered[...], planes, ((1,), (0,)))
+            denom = (base + DIFFUSION * wave_y[0:1, n * 256 : (n + 1) * 256]) + damping[:, 0:1]
             scaled = (modal / denom).astype(BF16)
             modes[:, n * 256 : (n + 1) * 256] = dot(synthesis[...], scaled, ((1,), (0,))).astype(BF16)
         solved[k] = dot(modes[...], table[...], ((1,), (0,))).astype(BF16)
@@ -292,7 +299,7 @@
         copy.wait_send()
 
 
-def spectral_step(deposit, thermal, table, analysis, synthesis, damping, wave_y):
+def spectral_step(deposit, thermal, table, analysis, synthesis, decay, wave_y):
     any_space, vmem = pl.BlockSpec(memory_space=pl.ANY), pl.BlockSpec(memory_space=pltpu.VMEM)
     return pl.pallas_call(
         spectral_kernel,
@@ -300,6 +307,8 @@
         in_specs=[any_space, any_space, vmem, vmem, vmem, vmem, vmem],
         out_specs=any_space,
         scratch_shapes=[
+            pltpu.VMEM((NZ, NZ), BF16),
+            pltpu.VMEM((NZ, LANES), F32),
             pltpu.VMEM((CZ + 2, CY + 16, NX), F32),
             pltpu.VMEM((CZ, CY, NX), F32),
             pltpu.VMEM((CZ * CY, NX), BF16),
@@ -333,7 +342,7 @@
             collective_id=0, has_side_effects=True, vmem_limit_bytes=60 * 2**20
         ),
         name="spectral_step",
-    )(deposit, thermal, table, analysis, synthesis, damping, wave_y)
+    )(deposit, thermal, table, analysis, synthesis, decay, wave_y)
 
 
 def home_kernel(home, table, out):
@@ -372,21 +381,15 @@
     one, nil = jnp.ones((LANES, LANES), BF16), jnp.zeros((LANES, LANES), BF16)
 
     def tile(group, start):
-        chosen, high, rest = [], [], []
+        chosen, weights = [], []
         for n in range(WINDOW):
             key, heat = key_rows[pl.ds(start + n, 1), :], energy_rows[pl.ds(start + n, 1), :]
             hit = lane == (key & (LANES - 1)).astype(F32).astype(BF16)
-            top = heat.astype(BF16)
-            high.append(jnp.where(hit, top, nil))
-            rest.append(jnp.where(hit, (heat - top.astype(F32)).astype(BF16), nil))
+            weights.append(jnp.where(hit, heat.astype(BF16), nil))
             line = (key >> 7) - group * CY
             line = jnp.where((line >= 0) & (line < CY), line, -1).astype(F32).astype(BF16)
             chosen.append(jnp.where(lane == line, one, nil))
-        weights = jnp.concatenate(
-            [jnp.concatenate(high, axis=1), jnp.concatenate(rest, axis=1)], axis=0
-        )
-        sums = dot(jnp.concatenate(chosen, axis=1), weights, ((1,), (1,)))
-        return sums[:, :LANES] + sums[:, LANES:]
+        return dot(jnp.concatenate(chosen, axis=1), jnp.concatenate(weights, axis=1), ((1,), (1,)))
 
     per_level = NX // LANES
     starts = [first[level * per_level + n] for n in range(per_level)]
@@ -408,7 +411,6 @@
     x = location[0]
     key = ((location[2] * (NX // LANES) + x // LANES) * CY + location[1]) * LANES + x % LANES
     key = jnp.where(live, key, GROUPS * CY * LANES)
-    energy = jnp.where(live, energy, 0.0)
     key, energy = lax.sort((key, energy), num_keys=1, is_stable=False)
     key, energy = key.reshape(-1, LANES), energy.reshape(-1, LANES)
     group = jnp.arange(GROUPS, dtype=jnp.int32)[:, None] * (CY * LANES)
@@ -433,11 +435,10 @@
 def body(thermal, location, energy, tally, decay, analysis, synthesis):
     deposit = deposit_step(location, energy, tally)
     table = jnp.asarray(cas_table(NX))
-    analysis = analysis.reshape(NZ, COLS, PARTS, QUAD).transpose(0, 2, 1, 3).reshape(NZ, NZ)
     index = np.arange(NY)
     wave_y = ((np.minimum(index, NY - index) * (2.0 * math.pi / NY)) ** 2).astype(np.float32)
     home = spectral_step(
-        deposit, thermal, table, analysis, synthesis, decay[:, None], jnp.asarray(wave_y)[None, :]
+        deposit, thermal, table, analysis, synthesis, decay[None, :], jnp.asarray(wave_y)[None, :]
     )
     ordered = cas_table(NX).reshape(DEVICES, OWN, NX).transpose(1, 0, 2).reshape(NX, NX)
     return home_step(home, jnp.asarray(ordered))

time: 191 us -> 172 us (0.901)
  Pallas kernels: 164 us -> 148 us
  local copies, waits for them, and re-layouts: 3.63 us -> 0.31 us
    pallas_call x1, Pallas kernels: 22.8 us -> 13.6 us  [deposit_step(): pl.pallas_call(deposit_kernel, out_shape=jax.ShapeDtypeStruct((CZ, CY, NX...]
    pallas_call x1, Pallas kernels: 133 us -> 126 us  [spectral_step(): pl.pallas_call(spectral_kernel, out_shape=jax.ShapeDtypeStruct((CZ, CY, N...]
where the time goes in v3:
time: 172 us; the launch traced here: 171 us
  Pallas kernels  148 us (86%)
  other arithmetic  22.7 us (13%)
    pallas_call x1, Pallas kernels, spectral_step(): pl.pallas_call(spectral_kernel, out_shape=jax.ShapeDtypeStruct((CZ, CY, N...  126 us
    sort x1, other arithmetic, deposit_step(): key, energy = lax.sort((key, energy), num_keys=1, is_stable=False)  19.1 us
    pallas_call x1, Pallas kernels, deposit_step(): pl.pallas_call(deposit_kernel, out_shape=jax.ShapeDtypeStruct((CZ, CY, NX...  13.6 us
    pallas_call x1, Pallas kernels, home_step(): pl.pallas_call(home_kernel, grid=(CZ // QUAD,), out_shape=jax.ShapeDtypeS...  8.4 us

profile of v3, /device:TPU:1, one launch (start us, length us, event | category | flops | bytes accessed | tf_op | source)
XLA Modules:
  0.0 171.4 jit_solution(15293495748026395504)
XLA Ops:
  0.7 3.0 %fusion.10 = (s32[1,65536]{1,0:T(1,128)S(1)}, s32[1,65536]{1,0:T(1,128)S(1)}, s32[1,65536]{1,0:T(1,128)S(1)}) fusion(s32[3,65536]{1,0:T(4,128)} %param.11), kind=kLoop, calls=%fused_computation.24 | loop fusion | flops 65536 | bytes 1572864 | tf_op jit(solution)/shard_map/slice | solution.py:411
  3.7 0.3 fusion.5
  4.0 19.1 %sort.15 = (s32[65536]{0:T(1024)S(1)}, f32[65536]{0:T(1024)S(1)}) sort(s32[65536]{0:T(1024)S(1)} %fusion.5, f32[65536]{0:T(1024)} %param.12), dimensions={0}, to_apply=%region_0.1 | sort | flops 1048576 | bytes 1048576 | tf_op jit(solution)/shard_map/sort | solution.py:414
  23.1 0.3 slice_reduce_fusion
  23.4 0.2 convert_reduce_fusion
  23.6 13.6 %deposit_step.1.deposit = f32[16,128,1024]{2,1,0:T(8,128)} custom-call(s32[128]{0:T(128)S(1)} %get-tuple-element.15.first, s32[128]{0:T(128)S(1)} %get-tuple-element.14.last, s32[512,128]{1,0:T(8,128)S(1)} %bitcast.11, f32[512,128]{1,0:T(8,128)S(1)} %bitcast.12), custom_call_target="tpu_custom_call" | custom-call | tf_op jit(solution)/shard_map/deposit_step/pallas_call | solution.py:420
  37.3 0.0 copy-start
  37.3 125.7 %spectral_step.1 = bf16[16,128,1024]{2,1,0:T(8,128)(2,1)} custom-call(f32[16,128,1024]{2,1,0:T(8,128)} %deposit_step.1.deposit, f32[16,128,1024]{2,1,0:T(8,128)} %thermal.1, bf16[1024,1024]{1,0:T(8,128)(2,1)} %constant.42.clone.table, bf16[256,256]{1,0:T(8,128)(2,1)} %analysis.1, bf16[256,256]{1,0:T(8,128)(2,1)} %synthesis.1, f32[1,256]{1,0:T(1,128)} %bitcast.17, ...), custom_call_target="tpu_custom_call" | custom-call | tf_op jit(solution)/shard_map/spectral_step/pallas_call | solution.py:304
  163.0 0.0 copy-done
  163.0 8.4 %home_step.1 = f32[2048,1024]{1,0:T(8,128)} custom-call(bf16[2048,1024]{1,0:T(8,128)(2,1)} %bitcast.13, bf16[1024,1024]{1,0:T(8,128)(2,1)S(1)} %copy-done), custom_call_target="tpu_custom_call" | custom-call | tf_op jit(solution)/shard_map/home_step/pallas_call | solution.py:355
  (2 shorter events, 0.0 us)
Async XLA Ops:
  37.3 125.7 %copy-start = (bf16[1024,1024]{1,0:T(8,128)(2,1)S(1)}, bf16[1024,1024]{1,0:T(8,128)(2,1)}, u32[]{:S(2)}) copy-start(bf16[1024,1024]{1,0:T(8,128)(2,1)} %constant.44.clone.table) | copy-start | bytes 6291460

commit v4 on v3

--- a/solution.py
+++ b/solution.py
@@ -23,7 +23,7 @@
 PARTS = 4
 QUAD = CZ // PARTS
 MSG = QUAD * OWN
-PHASES = (0, 1, 3, 5, 7, 8)
+PHASES = (0, 1, 2, 4, 6, 7, 8)
 ORDER = (1, 2, 0, 3)
 LANES = 128
 WINDOW = 6

time: 172 us -> 172 us (level)
  no operation moved by 1% of the time
where the time goes in v4:
time: 172 us; the launch traced here: 171 us
  Pallas kernels  148 us (86%)
  other arithmetic  22.7 us (13%)
    pallas_call x1, Pallas kernels, spectral_step(): pl.pallas_call(spectral_kernel, out_shape=jax.ShapeDtypeStruct((CZ, CY, N...  126 us
    sort x1, other arithmetic, deposit_step(): key, energy = lax.sort((key, energy), num_keys=1, is_stable=False)  19.1 us
    pallas_call x1, Pallas kernels, deposit_step(): pl.pallas_call(deposit_kernel, out_shape=jax.ShapeDtypeStruct((CZ, CY, NX...  13.6 us
    pallas_call x1, Pallas kernels, home_step(): pl.pallas_call(home_kernel, grid=(CZ // QUAD,), out_shape=jax.ShapeDtypeS...  8.4 us

profile of v4, /device:TPU:1, one launch (start us, length us, event | category | flops | bytes accessed | tf_op | source)
XLA Modules:
  0.0 171.4 jit_solution(4892507972256796532)
XLA Ops:
  0.7 3.0 %fusion.10 = (s32[1,65536]{1,0:T(1,128)S(1)}, s32[1,65536]{1,0:T(1,128)S(1)}, s32[1,65536]{1,0:T(1,128)S(1)}) fusion(s32[3,65536]{1,0:T(4,128)} %param.11), kind=kLoop, calls=%fused_computation.24 | loop fusion | flops 65536 | bytes 1572864 | tf_op jit(solution)/shard_map/slice | solution.py:411
  3.7 0.3 fusion.5
  4.0 19.1 %sort.15 = (s32[65536]{0:T(1024)S(1)}, f32[65536]{0:T(1024)S(1)}) sort(s32[65536]{0:T(1024)S(1)} %fusion.5, f32[65536]{0:T(1024)} %param.12), dimensions={0}, to_apply=%region_0.1 | sort | flops 1048576 | bytes 1048576 | tf_op jit(solution)/shard_map/sort | solution.py:414
  23.1 0.3 slice_reduce_fusion
  23.4 0.2 convert_reduce_fusion
  23.6 13.6 %deposit_step.1.deposit = f32[16,128,1024]{2,1,0:T(8,128)} custom-call(s32[128]{0:T(128)S(1)} %get-tuple-element.15.first, s32[128]{0:T(128)S(1)} %get-tuple-element.14.last, s32[512,128]{1,0:T(8,128)S(1)} %bitcast.11, f32[512,128]{1,0:T(8,128)S(1)} %bitcast.12), custom_call_target="tpu_custom_call" | custom-call | tf_op jit(solution)/shard_map/deposit_step/pallas_call | solution.py:420
  37.3 0.0 copy-start
  37.3 125.7 %spectral_step.1 = bf16[16,128,1024]{2,1,0:T(8,128)(2,1)} custom-call(f32[16,128,1024]{2,1,0:T(8,128)} %deposit_step.1.deposit, f32[16,128,1024]{2,1,0:T(8,128)} %thermal.1, bf16[1024,1024]{1,0:T(8,128)(2,1)} %constant.42.clone.table, bf16[256,256]{1,0:T(8,128)(2,1)} %analysis.1, bf16[256,256]{1,0:T(8,128)(2,1)} %synthesis.1, f32[1,256]{1,0:T(1,128)} %bitcast.17, ...), custom_call_target="tpu_custom_call" | custom-call | tf_op jit(solution)/shard_map/spectral_step/pallas_call | solution.py:304
  163.0 0.0 copy-done
  163.0 8.4 %home_step.1 = f32[2048,1024]{1,0:T(8,128)} custom-call(bf16[2048,1024]{1,0:T(8,128)(2,1)} %bitcast.13, bf16[1024,1024]{1,0:T(8,128)(2,1)S(1)} %copy-done), custom_call_target="tpu_custom_call" | custom-call | tf_op jit(solution)/shard_map/home_step/pallas_call | solution.py:355
  (2 shorter events, 0.0 us)
Async XLA Ops:
  37.3 125.8 %copy-start = (bf16[1024,1024]{1,0:T(8,128)(2,1)S(1)}, bf16[1024,1024]{1,0:T(8,128)(2,1)}, u32[]{:S(2)}) copy-start(bf16[1024,1024]{1,0:T(8,128)(2,1)} %constant.44.clone.table) | copy-start | bytes 6291460
